TPU v7x, 512 devices: a whole 4x8x8 slice. The times are simulated.
512 devices in a mesh: dp: 64 (over z, x, core), mp: 8 (over y).
Axes of the slice: x: 4, y: 8, z: 8, core: 2. Of those that a mesh axis runs over, the one named last changes fastest.
Arguments:
- teacher_in: bfloat16 [64, 1024, 1408], P('dp', 'mp'), may hold values from -8 to 8
- teacher_gain: float32 [1408], replicated, may hold values from 0.5 to 1.5
- teacher_qkv: bfloat16 [3, 1408, 1408], P(None, 'mp'), may hold values from -1 to 1
- teacher_out: bfloat16 [1408, 1408], P('mp'), may hold values from -0.15625 to 0.15625
- student_in: bfloat16 [64, 1024, 1024], P('dp', None, 'mp'), may hold values from -6 to 6
- student_gain: float32 [1024], replicated, may hold values from 0.25 to 1.75
- widen_weight: bfloat16 [1024, 4096], P(None, 'mp'), may hold values from -0.1875 to 0.1875
- narrow_weight: bfloat16 [4096, 1024], P('mp'), may hold values from -0.09375 to 0.09375
- target_head: bfloat16 [1408, 1024], P('mp'), may hold values from -0.1875 to 0.1875
- positions: int32 [64, 512], P('dp'), may hold values from 0 to 1023, as said below
- counts: int32 [64], P('dp'), may hold values from 1 to 512, 16384 in all
Outputs:
- grad_widen: float32 [1024, 4096], P('dp', 'mp')
- grad_narrow: float32 [1024, 4096], P('dp', 'mp')
- losses: float32 [64], P('dp')
Inputs may be any that keep to these rules, and one draw needn't show every extreme that they name: `positions`: the entries of one image's list are distinct; only the first counts of them are live. The counts of all images sum to 16384.
All inputs are finite; a program needn't handle non-finite values. No bound on the sum of `counts` on one device may be relied on, other than what follows from the above.
Results may differ from a plain program's by a relative error of at most 0.02.
Values may be sent and summed in bfloat16 or wider, within the bound.
No kernel may reach another device: no remote copies, remote signals or barrier semaphores. Data moves between devices by JAX's collectives and lax.ppermute only.
A program may use at most 64 MiB of HBM per device.

v0:
```python
import jax
import jax.numpy as jnp
from jax import lax
from jax.sharding import PartitionSpec as P

TD = 1408
TH = 16
EPSILON = 1e-06


def in_order(tiles, dim):
    tiles = jnp.moveaxis(tiles, 0, dim)
    dims = tiles.shape
    return tiles.reshape(*dims[:dim], dims[dim] * dims[dim + 1], *dims[dim + 2 :])


def sent_to_all(array, axis):
    copies = jnp.broadcast_to(array, (lax.axis_size(axis), *array.shape))
    return lax.all_to_all(copies, axis, split_axis=0, concat_axis=0, tiled=True)


def gather_directly(array, axis, dim):
    return in_order(sent_to_all(array, axis), dim)


def rows_for(lines, peers):
    spare = -lines.shape[0] % peers
    if not spare:
        return lines
    return jnp.concatenate([lines, jnp.zeros((spare, *lines.shape[1:]), lines.dtype)])


def total_of(array, axis):
    lines = array.reshape(-1, *array.shape[1:][-1:])
    own = lax.psum_scatter(
        rows_for(lines, lax.axis_size(axis)), axis, scatter_dimension=0, tiled=True
    )
    whole = lax.all_gather(own, axis).reshape(-1, *lines.shape[1:])
    return lax.slice_in_dim(whole, 0, len(lines)).reshape(array.shape)


def of_everyone(array, axis):
    everything = sent_to_all(array, axis)
    return jnp.sum(everything, axis=0)


def packed_total(arrays, axis):
    ends = [0]
    for a in arrays:
        ends.append(ends[-1] + a.size)
    so_far = of_everyone(jnp.concatenate([a.ravel() for a in arrays]), axis)
    return tuple((so_far[b:e].reshape(a.shape) for a, b, e in zip(arrays, ends, ends[1:])))


def cut_along(array, dim, peers):
    dims = array.shape
    tiles = array.reshape(*dims[:dim], peers, dims[dim] // peers, *dims[dim + 1 :])
    return jnp.moveaxis(tiles, dim, 0)


def summed_on_arrival(array, axis, dim):
    peers = lax.axis_size(axis)
    tiles = lax.all_to_all(cut_along(array, dim, peers), axis, 0, 0, tiled=True)
    return jnp.sum(tiles, axis=0)


def layer_norm(values, gain):
    mean_val = jnp.mean(values, axis=-1, keepdims=True)
    centred = values - mean_val
    spread = jnp.mean(centred * centred, axis=-1, keepdims=True)
    return centred * lax.rsqrt(spread + EPSILON) * gain


def gelu_value(pre):
    return 0.5 * pre * (1.0 + lax.erf(pre * 0.7071067811865476))


def gelu_slope(pre):
    return 0.5 * (1.0 + lax.erf(pre * 0.7071067811865476)) + pre * 0.3989422804014327 * jnp.exp(
        -0.5 * pre * pre
    )


def on_device(
    teacher_in,
    teacher_gain,
    teacher_qkv,
    teacher_out,
    student_in,
    student_gain,
    widen_weight,
    narrow_weight,
    target_head,
    positions,
    counts,
):
    patches_local = teacher_in[0]
    slot_total = positions.shape[1]
    picked = positions[0]
    live_count = counts[0]
    head_size = TD // TH
    factor = head_size ** (-0.5)
    local_width = teacher_qkv.shape[1]
    local_heads = local_width // head_size
    gathered = lax.all_gather(patches_local, "mp", axis=0, tiled=True)
    teach_normed = layer_norm(gathered.astype(jnp.float32), teacher_gain).astype(jnp.bfloat16)
    key_rows = jnp.einsum(
        "pi,oi->po", teach_normed, teacher_qkv[1], preferred_element_type=jnp.float32
    ).astype(jnp.bfloat16)
    value_rows = jnp.einsum(
        "pi,oi->po", teach_normed, teacher_qkv[2], preferred_element_type=jnp.float32
    ).astype(jnp.bfloat16)
    query_rows = jnp.einsum(
        "pi,oi->po", teach_normed[picked], teacher_qkv[0], preferred_element_type=jnp.float32
    ).astype(jnp.bfloat16)
    query_heads = query_rows.reshape(slot_total, local_heads, head_size)
    key_heads = key_rows.reshape(-1, local_heads, head_size)
    value_heads = value_rows.reshape(-1, local_heads, head_size)
    scores = (
        jnp.einsum("shd,phd->hsp", query_heads, key_heads, preferred_element_type=jnp.float32)
        * factor
    )
    largest = jnp.max(scores, axis=-1, keepdims=True)
    soft_num = jnp.exp(scores - largest)
    soft_weights = (soft_num / jnp.sum(soft_num, axis=-1, keepdims=True)).astype(jnp.bfloat16)
    attended = jnp.einsum(
        "hsp,phd->shd", soft_weights, value_heads, preferred_element_type=jnp.float32
    )
    attended = attended.astype(jnp.bfloat16).reshape(slot_total, local_width)
    blended = jnp.einsum(
        "sw,ow->so",
        gather_directly(attended, "mp", 1),
        teacher_out,
        preferred_element_type=jnp.float32,
    )
    own_start = lax.axis_index("mp") * local_width
    residual_part = lax.dynamic_slice_in_dim(gathered[picked], own_start, local_width, 1)
    targets = (residual_part.astype(jnp.float32) + blended).astype(jnp.bfloat16)
    slot_ids = jnp.arange(slot_total, dtype=jnp.int32)
    row_weight = jnp.where(
        slot_ids < live_count, 1.0 / live_count.astype(jnp.float32), jnp.zeros((), jnp.float32)
    )
    student_rows = student_in[0][picked]
    student_full = gather_directly(student_rows, "mp", 1)
    student_f32 = student_full.astype(jnp.float32)
    normed_rows = layer_norm(student_f32, student_gain).astype(jnp.bfloat16)
    pre_act = jnp.dot(normed_rows, widen_weight, preferred_element_type=jnp.float32)
    activity = gelu_value(pre_act).astype(jnp.bfloat16)
    branch_sum = total_of(
        jnp.dot(activity, narrow_weight, preferred_element_type=jnp.float32).astype(jnp.bfloat16),
        "mp",
    ).astype(jnp.float32)
    outputs = (student_f32 + branch_sum).astype(jnp.bfloat16)
    predicted = jnp.einsum("rd,cd->rc", outputs, target_head, preferred_element_type=jnp.float32)
    targets32 = targets.astype(jnp.float32)
    inner_sum, pred_sq, target_sq = packed_total(
        (
            jnp.sum(predicted * targets32, axis=-1),
            jnp.sum(predicted * predicted, axis=-1),
            jnp.sum(targets32 * targets32, axis=-1),
        ),
        "mp",
    )
    inv_pred = lax.rsqrt(pred_sq + EPSILON)
    inv_target = lax.rsqrt(target_sq + EPSILON)
    cosine = inner_sum * inv_pred * inv_target
    row_loss = row_weight * (1.0 - cosine)
    pred_slope = (row_weight * cosine * inv_pred * inv_pred)[:, None] * predicted - (
        row_weight * inv_pred * inv_target
    )[:, None] * targets32
    pred_slope = pred_slope.astype(jnp.bfloat16)
    back_sum = lax.psum(
        jnp.einsum("rc,cd->rd", pred_slope, target_head, preferred_element_type=jnp.float32).astype(
            jnp.bfloat16
        ),
        "mp",
    )
    back_act = jnp.einsum("rd,hd->rh", back_sum, narrow_weight, preferred_element_type=jnp.float32)
    back_pre = (back_act * gelu_slope(pre_act)).astype(jnp.bfloat16)
    column_part = normed_rows
    grad_widen = summed_on_arrival(
        jnp.einsum("rd,rh->dh", column_part, back_pre, preferred_element_type=jnp.float32), "dp", 0
    )
    column_part = back_sum
    grad_narrow = summed_on_arrival(
        jnp.einsum("rd,rh->dh", column_part, activity, preferred_element_type=jnp.float32), "dp", 0
    )
    image_loss = jnp.sum(row_loss)
    return (grad_widen, grad_narrow, jnp.reshape(image_loss, (1,)))


def solution(mesh):
    placed = (
        P("dp", "mp", None),
        P(),
        P(None, "mp", None),
        P("mp", None),
        P("dp", None, "mp"),
        P(),
        P(None, "mp"),
        P("mp", None),
        P("mp", None),
        P("dp", None),
        P("dp"),
    )
    return jax.shard_map(
        on_device,
        mesh=mesh,
        in_specs=placed,
        out_specs=(P("dp", "mp"), P("dp", "mp"), P("dp")),
        check_vma=False,
    )
```

profile of v0, /device:TPU:2, one launch (start us, length us, event | category | flops | bytes accessed | tf_op | source)
XLA Modules:
  0.0 403.2 jit_solution(8823197058762961276)
XLA Ops:
  7.2 0.7 all-gather.7.cloned.1.call-update
  8.0 0.7 compare_select_fusion
  8.7 2.0 gather_fusion
  10.9 42.5 %all_to_all.26 = bf16[8,512,128]{1,2,0:T(8,128)(2,1)S(1)} all-to-all(bf16[8,512,128]{1,2,0:T(8,128)(2,1)S(1)} %broadcast_in_dim.14), channel_id=1, replica_groups=mesh['dp'=64,'mp'=8] {'mp'}, dimensions={0} | all-to-all | bytes 2097152 | tf_op jit(solution)/shard_map/all_to_all | solution.py:19
  53.6 0.3 fusion.10
  54.0 0.3 fusion.13
  54.3 0.3 copy-done.13
  54.6 1.7 multiply_convert_fusion
  56.4 0.8 copy-done.9
  57.2 1.7 convolution_convert_fusion.1
  58.9 13.3 %all-gather.7.cloned.1.call-done = bf16[1,1024,1408]{2,1,0:T(8,128)(2,1)} async-done(((bf16[1,128,1408]{2,1,0:T(8,128)(2,1)}), bf16[1,1024,1408]{2,1,0:T(8,128)(2,1)}) %all-gather.7.cloned.1.call-update) | async-done | bytes 2883600 | tf_op jit(solution)/shard_map/all_gather | solution.py:105
  72.1 2.4 convert_reduce_fusion
  74.6 0.2 copy-done.1
  74.8 0.9 fusion.3
  75.7 2.5 fusion.5
  78.2 5.5 %gather_fusion.2 = bf16[512,1408]{1,0:T(8,128)(2,1)S(1)} fusion(bf16[1024,1408]{1,0:T(8,128)(2,1)} %fusion.5, s32[1024]{0:T(1024)S(1)} %pad_clamp_fusion), kind=kCustom, calls=%fused_computation.2 | custom fusion | bytes 2885632 | tf_op jit(solution)/shard_map/gather | solution.py:114
  83.8 2.4 convolution_convert_fusion.4
  86.2 3.1 convolution_convert_fusion.2
  89.3 1.1 convolution_convert_fusion.3
  90.4 3.4 fusion.52
  93.8 3.0 fusion.21
  96.8 1.2 broadcast_in_dim.17
  98.1 4.2 %all-to-all-start.1 = ((bf16[8,512,176]{1,2,0:T(8,128)(2,1)}), bf16[8,512,176]{1,2,0:T(8,128)(2,1)S(1)}, u32[]{:S(2)}, u32[]{:S(2)}) async-start(bf16[8,512,176]{1,2,0:T(8,128)(2,1)} %broadcast_in_dim.17), calls=%async_computation.1 | async-start | bytes 2883584 | tf_op jit(solution)/shard_map/all_to_all | solution.py:19
  102.3 0.2 all-gather.5.cloned.1.call-start
  102.5 22.0 %reduce-scatter.4.cloned.1.call-done = bf16[64,1024]{1,0:T(8,128)(2,1)} async-done(((bf16[512,1024]{1,0:T(8,128)(2,1)}), bf16[64,1024]{1,0:T(8,128)(2,1)}) %reduce-scatter.4.cloned.1.call-update) | async-done | bytes 131088 | tf_op jit(solution)/shard_map/reduce_scatter | solution.py:35
  124.6 6.3 %gather_fusion.1 = bf16[512,1408]{1,0:T(8,128)(2,1)} fusion(bf16[1024,1408]{1,0:T(8,128)(2,1)} %bitcast.75, s32[1024]{0:T(1024)S(1)} %pad_clamp_fusion), kind=kCustom, calls=%fused_computation.1 | custom fusion | bytes 2885632 | tf_op jit(solution)/shard_map/gather | solution.py:137
  130.9 1.9 constant_dynamic-slice_fusion
  132.7 1.7 copy.42
  134.5 35.3 %all-gather.5.cloned.1.call-done = bf16[512,1024]{1,0:T(8,128)(2,1)} async-done(((bf16[64,1024]{1,0:T(8,128)(2,1)}), bf16[512,1024]{1,0:T(8,128)(2,1)}) %all-gather.5.cloned.1.call-update) | async-done | bytes 1048592 | tf_op jit(solution)/shard_map/all_gather | solution.py:38
  169.7 2.3 copy.36
  172.0 2.5 fusion.14
  174.5 1.6 fusion.20
  176.2 0.4 multiply_reduce_fusion.3
  176.6 0.3 copy-done.4
  176.9 0.6 broadcast_in_dim.18
  177.6 4.3 %all-to-all-start.2 = ((f32[8,1,1536]{2,1,0:T(1,128)}), f32[8,1,1536]{2,1,0:T(1,128)S(1)}, u32[]{:S(2)}, u32[]{:S(2)}) async-start(f32[8,1,1536]{2,1,0:T(1,128)} %broadcast_in_dim.18), calls=%async_computation.2 | async-start | bytes 98304 | tf_op jit(solution)/shard_map/all_to_all | solution.py:19
  182.6 7.5 %all-to-all-done.2 = f32[8,1,1536]{2,1,0:T(1,128)S(1)} async-done(((f32[8,1,1536]{2,1,0:T(1,128)}), f32[8,1,1536]{2,1,0:T(1,128)S(1)}, u32[]{:S(2)}, u32[]{:S(2)}) %all-to-all-start.2) | async-done | bytes 49184 | tf_op jit(solution)/shard_map/all_to_all | solution.py:19
  190.1 0.6 fusion.43
  190.8 2.5 convolution_convert_fusion
  193.3 77.6 %all-reduce.2.cloned.1.call-done = bf16[512,1024]{1,0:T(8,128)(2,1)} async-done(((bf16[512,1024]{1,0:T(8,128)(2,1)}), bf16[512,1024]{1,0:T(8,128)(2,1)}) %all-reduce.2.cloned.1.call-update) | async-done | bytes 1048592 | tf_op jit(solution)/shard_map/psum | solution.py:172
  270.9 4.4 %fusion.22 = f32[64,16,512]{2,1,0:T(8,128)} fusion(bf16[64,16,512]{2,1,0:T(8,128)(2,1)S(1)} %bitcast.78, bf16[512,1024]{1,0:T(8,128)(2,1)} %all-reduce.2.cloned.1.call-done, bf16[512,1024]{1,0:T(8,128)(2,1)S(1)} %copy-done, f32[512,512]{1,0:T(8,128)} %get-tuple-element.13), kind=kOutput, calls=%fused_computation.40 | convolution fusion | flops 1076363264 | bytes 6291456 | tf_op jit(solution)/shard_map/rd,rh->dh/dot_general | solution.py:182
  275.3 10.9 %all-to-all-start.3 = ((f32[64,16,512]{2,1,0:T(8,128)}), f32[64,16,512]{2,1,0:T(8,128)S(1)}, u32[]{:S(2)}, u32[]{:S(2)}) async-start(f32[64,16,512]{2,1,0:T(8,128)} %fusion.22), calls=%async_computation.3 | async-start | bytes 4194304 | tf_op jit(solution)/shard_map/all_to_all | solution.py:63
  286.3 3.4 fusion.53
  289.7 47.9 %all-to-all-done.3 = f32[64,16,512]{2,1,0:T(8,128)S(1)} async-done(((f32[64,16,512]{2,1,0:T(8,128)}), f32[64,16,512]{2,1,0:T(8,128)S(1)}, u32[]{:S(2)}, u32[]{:S(2)}) %all-to-all-start.3) | async-done | bytes 2097184 | tf_op jit(solution)/shard_map/all_to_all | solution.py:63
  337.5 5.6 %all-to-all-start.4 = ((f32[64,16,512]{2,1,0:T(8,128)}), f32[64,16,512]{2,1,0:T(8,128)}, u32[]{:S(2)}, u32[]{:S(2)}) async-start(f32[64,16,512]{2,1,0:T(8,128)} %bitcast.21), calls=%async_computation.4 | async-start | bytes 4194304 | tf_op jit(solution)/shard_map/all_to_all | solution.py:63
  343.2 0.8 reduce_sum.117
  343.9 50.4 %all-to-all-done.4 = f32[64,16,512]{2,1,0:T(8,128)} async-done(((f32[64,16,512]{2,1,0:T(8,128)}), f32[64,16,512]{2,1,0:T(8,128)}, u32[]{:S(2)}, u32[]{:S(2)}) %all-to-all-start.4) | async-done | bytes 2097184 | tf_op jit(solution)/shard_map/all_to_all | solution.py:63
  394.3 2.3 reduce_sum.118
  (44 shorter events, 0.7 us)
Async XLA Ops:
  7.2 50.0 %copy-start = (bf16[512,1024]{1,0:T(8,128)(2,1)S(1)}, bf16[512,1024]{1,0:T(8,128)(2,1)}, u32[]{:S(2)}) copy-start(bf16[512,1024]{1,0:T(8,128)(2,1)} %param.18) | copy-start | bytes 3145732
  7.2 65.0 %all-gather.7.cloned.1.call-start = ((), (), s32[]{:S(2)}) async-start(), calls=%async_computation.8 | async-start | bytes 3244032 | tf_op jit(solution)/shard_map/all_gather | solution.py:105
  7.9 116.6 %reduce-scatter.4.cloned.1.call-start = ((), (), s32[]{:S(2)}) async-start(), calls=%async_computation.9 | async-start | bytes 1179648 | tf_op jit(solution)/shard_map/reduce_scatter | solution.py:35
  10.9 43.1 %copy-start.11 = (f32[1024]{0:T(1024)S(1)}, f32[1024]{0:T(1024)}, u32[]{:S(2)}) copy-start(f32[1024]{0:T(1024)} %param.16) | copy-start | bytes 12292
  53.4 1.2 copy-start.13
  54.6 1.7 copy-start.7
  56.4 0.8 copy-start.9
  72.1 2.7 copy-start.1
  74.5 1.2 copy-start.10
  83.8 2.5 copy-start.12
  86.2 3.1 copy-start.2
  89.3 1.1 copy-start.14
  98.1 76.4 %all-to-all-start.1 = ((bf16[8,512,176]{1,2,0:T(8,128)(2,1)}), bf16[8,512,176]{1,2,0:T(8,128)(2,1)S(1)}, u32[]{:S(2)}, u32[]{:S(2)}) async-start(bf16[8,512,176]{1,2,0:T(8,128)(2,1)} %broadcast_in_dim.17), calls=%async_computation.1 | async-start | bytes 2883584 | tf_op jit(solution)/shard_map/all_to_all | solution.py:19
  102.3 67.4 %all-gather.5.cloned.1.call-start = ((), (), s32[]{:S(2)}) async-start(), calls=%async_computation.7 | async-start | bytes 1179648 | tf_op jit(solution)/shard_map/all_gather | solution.py:38
  174.5 1.6 copy-start.3
  174.5 1.6 copy-start.5
  176.2 0.8 copy-start.4
  176.2 14.6 %copy-start.6 = (bf16[176,1024]{1,0:T(8,128)(2,1)S(1)}, bf16[176,1024]{1,0:T(8,128)(2,1)}, u32[]{:S(2)}) copy-start(bf16[176,1024]{1,0:T(8,128)(2,1)} %param.19) | copy-start | bytes 1081348
  176.9 94.0 %copy-start.8 = (bf16[512,1024]{0,1:T(8,128)(2,1)S(1)}, bf16[512,1024]{0,1:T(8,128)(2,1)}, u32[]{:S(2)}) copy-start(bf16[512,1024]{0,1:T(8,128)(2,1)} %copy-done.7) | copy-start | bytes 3145732
  177.6 12.5 %all-to-all-start.2 = ((f32[8,1,1536]{2,1,0:T(1,128)}), f32[8,1,1536]{2,1,0:T(1,128)S(1)}, u32[]{:S(2)}, u32[]{:S(2)}) async-start(f32[8,1,1536]{2,1,0:T(1,128)} %broadcast_in_dim.18), calls=%async_computation.2 | async-start | bytes 98304 | tf_op jit(solution)/shard_map/all_to_all | solution.py:19
  181.9 89.0 %all-reduce.2.cloned.1.call-start = ((), (), s32[]{:S(2)}) async-start(), calls=%async_computation.6 | async-start | bytes 2097152 | tf_op jit(solution)/shard_map/psum | solution.py:172
  275.3 62.2 %all-to-all-start.3 = ((f32[64,16,512]{2,1,0:T(8,128)}), f32[64,16,512]{2,1,0:T(8,128)S(1)}, u32[]{:S(2)}, u32[]{:S(2)}) async-start(f32[64,16,512]{2,1,0:T(8,128)} %fusion.22), calls=%async_computation.3 | async-start | bytes 4194304 | tf_op jit(solution)/shard_map/all_to_all | solution.py:63
  337.5 56.8 %all-to-all-start.4 = ((f32[64,16,512]{2,1,0:T(8,128)}), f32[64,16,512]{2,1,0:T(8,128)}, u32[]{:S(2)}, u32[]{:S(2)}) async-start(f32[64,16,512]{2,1,0:T(8,128)} %bitcast.21), calls=%async_computation.4 | async-start | bytes 4194304 | tf_op jit(solution)/shard_map/all_to_all | solution.py:63
Sparse Core Ops, SparseCore 0:
  10.1 61.9 all-gather.6
  75.0 49.5 reduce-scatter.3
  126.6 43.0 all-gather.4
  193.4 77.4 all-reduce.1
where the time goes:
time: 404 us; the launch traced here: 403 us
  waiting for transfers between devices  255 us (63%)
  blocking collectives  42.5 us (11%)
  matrix products  28.7 us (7%)
  starting transfers between devices  25.4 us (6%)
  local copies, waits for them, and re-layouts  23.6 us (6%)
  between operations  14.7 us (4%)
  other arithmetic  13.6 us (3%)
    all_to_all x2, waiting for transfers between devices, summed_on_arrival(): tiles = lax.all_to_all(cut_along(array, dim, peers), axis, 0, 0, tiled=True)  98.3 us
    psum x1, waiting for transfers between devices, on_device(): lax.psum(jnp.einsum('rc,cd->rd', pred_slope, target_head, preferred_eleme...  77.6 us
    all_to_all x1, blocking collectives, sent_to_all(): return lax.all_to_all(copies, axis, split_axis=0, concat_axis=0, tiled=True)  42.5 us
    all_gather x1, waiting for transfers between devices, total_of(): whole = lax.all_gather(own, axis).reshape(-1, *lines.shape[1:])  35.3 us
    reduce_scatter x1, waiting for transfers between devices, total_of(): lax.psum_scatter(rows_for(lines, lax.axis_size(axis)), axis, scatter_dime...  22 us
    all_to_all x2, starting transfers between devices, summed_on_arrival(): tiles = lax.all_to_all(cut_along(array, dim, peers), axis, 0, 0, tiled=True)  16.5 us
    all_gather x1, waiting for transfers between devices, on_device(): gathered = lax.all_gather(patches_local, 'mp', axis=0, tiled=True)  13.3 us
    all_to_all x2, starting transfers between devices, sent_to_all(): return lax.all_to_all(copies, axis, split_axis=0, concat_axis=0, tiled=True)  8.57 us
  transfers between devices with their start and end apart: 8, of which 7 were waited for; matrix products, arithmetic and copies ran while one was open for 13% of the time, Pallas kernels for 0%

commit v1 on v0

--- a/solution.py
+++ b/solution.py
@@ -6,6 +6,10 @@
 TD = 1408
 TH = 16
 EPSILON = 1e-06
+
+
+def raise_cards(a0, mesh_dim="mp"):
+    return jnp.sum(jax.lax.all_gather(a0, mesh_dim), axis=0)
 
 
 def in_order(tiles, dim):
@@ -169,11 +173,10 @@
         row_weight * inv_pred * inv_target
     )[:, None] * targets32
     pred_slope = pred_slope.astype(jnp.bfloat16)
-    back_sum = lax.psum(
+    back_sum = raise_cards(
         jnp.einsum("rc,cd->rd", pred_slope, target_head, preferred_element_type=jnp.float32).astype(
             jnp.bfloat16
-        ),
-        "mp",
+        )
     )
     back_act = jnp.einsum("rd,hd->rh", back_sum, narrow_weight, preferred_element_type=jnp.float32)
     back_pre = (back_act * gelu_slope(pre_act)).astype(jnp.bfloat16)

time: 404 us -> 425 us (1.052)
  waiting for transfers between devices: 255 us -> 268 us
  other arithmetic: 13.6 us -> 19.4 us
    all_gather x0 -> x1, waiting for transfers between devices: none -> 93 us  [raise_cards(): return jnp.sum(jax.lax.all_gather(a0, mesh_dim), axis=0)]
    psum x1 -> x0, waiting for transfers between devices: 77.6 us -> none  [on_device(): lax.psum(jnp.einsum('rc,cd->rd', pred_slope, target_head, preferred_eleme...]
    reduce_sum x0 -> x1, other arithmetic: none -> 5.75 us  [raise_cards(): return jnp.sum(jax.lax.all_gather(a0, mesh_dim), axis=0)]
where the time goes in v1:
time: 425 us; the launch traced here: 424 us
  waiting for transfers between devices  268 us (63%)
  blocking collectives  42.5 us (10%)
  matrix products  28.8 us (7%)
  local copies, waits for them, and re-layouts  25.9 us (6%)
  starting transfers between devices  25.4 us (6%)
  other arithmetic  19.4 us (5%)
  between operations  14.7 us (3%)
    all_to_all x2, waiting for transfers between devices, summed_on_arrival(): tiles = lax.all_to_all(cut_along(array, dim, peers), axis, 0, 0, tiled=True)  96 us
    all_gather x1, waiting for transfers between devices, raise_cards(): return jnp.sum(jax.lax.all_gather(a0, mesh_dim), axis=0)  93 us
    all_to_all x1, blocking collectives, sent_to_all(): return lax.all_to_all(copies, axis, split_axis=0, concat_axis=0, tiled=True)  42.5 us
    all_gather x1, waiting for transfers between devices, total_of(): whole = lax.all_gather(own, axis).reshape(-1, *lines.shape[1:])  35 us
    reduce_scatter x1, waiting for transfers between devices, total_of(): lax.psum_scatter(rows_for(lines, lax.axis_size(axis)), axis, scatter_dime...  22.3 us
    all_to_all x2, starting transfers between devices, summed_on_arrival(): tiles = lax.all_to_all(cut_along(array, dim, peers), axis, 0, 0, tiled=True)  16.5 us
    all_gather x1, waiting for transfers between devices, on_device(): gathered = lax.all_gather(patches_local, 'mp', axis=0, tiled=True)  13.2 us
    all_to_all x2, starting transfers between devices, sent_to_all(): return lax.all_to_all(copies, axis, split_axis=0, concat_axis=0, tiled=True)  8.57 us
  transfers between devices with their start and end apart: 8, of which 7 were waited for; matrix products, arithmetic and copies ran while one was open for 13% of the time, Pallas kernels for 0%

profile of v1, /device:TPU:2, one launch (start us, length us, event | category | flops | bytes accessed | tf_op | source)
XLA Modules:
  0.0 424.4 jit_solution(818488090292904712)
XLA Ops:
  7.2 0.7 all-gather.9.cloned.1.call-update
  8.0 0.7 compare_select_fusion
  8.7 2.0 gather_fusion
  10.9 42.5 %all_to_all.26 = bf16[8,512,128]{1,2,0:T(8,128)(2,1)S(1)} all-to-all(bf16[8,512,128]{1,2,0:T(8,128)(2,1)S(1)} %broadcast_in_dim.14), channel_id=1, replica_groups=mesh['dp'=64,'mp'=8] {'mp'}, dimensions={0} | all-to-all | bytes 2097152 | tf_op jit(solution)/shard_map/all_to_all | solution.py:23
  53.6 0.3 fusion.10
  54.0 0.3 fusion.13
  54.3 0.3 copy-done.14
  54.6 1.8 multiply_convert_fusion
  56.5 0.8 copy-done.10
  57.3 1.7 convolution_convert_fusion.1
  59.0 13.2 %all-gather.9.cloned.1.call-done = bf16[1,1024,1408]{2,1,0:T(8,128)(2,1)} async-done(((bf16[1,128,1408]{2,1,0:T(8,128)(2,1)}), bf16[1,1024,1408]{2,1,0:T(8,128)(2,1)}) %all-gather.9.cloned.1.call-update) | async-done | bytes 2883600 | tf_op jit(solution)/shard_map/all_gather | solution.py:109
  72.1 2.4 convert_reduce_fusion
  74.8 0.9 fusion.3
  75.7 2.5 fusion.5
  78.2 5.5 %gather_fusion.2 = bf16[512,1408]{1,0:T(8,128)(2,1)S(1)} fusion(bf16[1024,1408]{1,0:T(8,128)(2,1)} %fusion.5, s32[1024]{0:T(1024)S(1)} %pad_clamp_fusion), kind=kCustom, calls=%fused_computation.2 | custom fusion | bytes 2885632 | tf_op jit(solution)/shard_map/gather | solution.py:118
  83.8 2.5 convolution_convert_fusion.4
  86.2 3.1 convolution_convert_fusion.2
  89.3 1.1 convolution_convert_fusion.3
  90.4 3.4 fusion.54
  93.8 3.0 fusion.21
  96.8 1.2 broadcast_in_dim.17
  98.1 4.2 all-to-all-start.1
  102.5 22.3 %reduce-scatter.4.cloned.1.call-done = bf16[64,1024]{1,0:T(8,128)(2,1)} async-done(((bf16[512,1024]{1,0:T(8,128)(2,1)}), bf16[64,1024]{1,0:T(8,128)(2,1)}) %reduce-scatter.4.cloned.1.call-update) | async-done | bytes 131088 | tf_op jit(solution)/shard_map/reduce_scatter | solution.py:39
  124.8 6.3 %gather_fusion.1 = bf16[512,1408]{1,0:T(8,128)(2,1)} fusion(bf16[1024,1408]{1,0:T(8,128)(2,1)} %bitcast.79, s32[1024]{0:T(1024)S(1)} %pad_clamp_fusion), kind=kCustom, calls=%fused_computation.1 | custom fusion | bytes 2885632 | tf_op jit(solution)/shard_map/gather | solution.py:141
  131.1 1.9 constant_dynamic-slice_fusion
  133.0 1.7 copy.46
  134.7 35.0 %all-gather.7.cloned.1.call-done = bf16[512,1024]{1,0:T(8,128)(2,1)} async-done(((bf16[64,1024]{1,0:T(8,128)(2,1)}), bf16[512,1024]{1,0:T(8,128)(2,1)}) %all-gather.7.cloned.1.call-update) | async-done | bytes 1048592 | tf_op jit(solution)/shard_map/all_gather | solution.py:42
  169.7 2.3 copy.39
  172.0 2.5 fusion.14
  174.5 1.6 fusion.20
  176.2 0.4 multiply_reduce_fusion.3
  176.6 0.3 copy-done.5
  176.9 0.6 broadcast_in_dim.18
  177.5 4.3 %all-to-all-start.2 = ((f32[8,1,1536]{2,1,0:T(1,128)}), f32[8,1,1536]{2,1,0:T(1,128)S(1)}, u32[]{:S(2)}, u32[]{:S(2)}) async-start(f32[8,1,1536]{2,1,0:T(1,128)} %broadcast_in_dim.18), calls=%async_computation.2 | async-start | bytes 98304 | tf_op jit(solution)/shard_map/all_to_all | solution.py:23
  182.6 7.5 %all-to-all-done.2 = f32[8,1,1536]{2,1,0:T(1,128)S(1)} async-done(((f32[8,1,1536]{2,1,0:T(1,128)}), f32[8,1,1536]{2,1,0:T(1,128)S(1)}, u32[]{:S(2)}, u32[]{:S(2)}) %all-to-all-start.2) | async-done | bytes 49184 | tf_op jit(solution)/shard_map/all_to_all | solution.py:23
  190.1 0.6 fusion.45
  190.7 2.4 convolution_convert_fusion
  193.2 93.0 %all-gather.11.cloned.1.call-done = bf16[4096,1024]{1,0:T(8,128)(2,1)} async-done(((bf16[512,1024]{1,0:T(8,128)(2,1)}), bf16[4096,1024]{1,0:T(8,128)(2,1)}) %all-gather.11.cloned.1.call-update) | async-done | bytes 8388624 | tf_op jit(solution)/shard_map/all_gather | solution.py:12
  286.2 5.8 %reduce_sum.129 = bf16[512,1024]{1,0:T(8,128)(2,1)S(1)} reduce(bf16[8,512,1024]{2,1,0:T(8,128)(2,1)} %bitcast.80, bf16[]{:T(256)} %constant.15.clone.1), dimensions={0}, to_apply=%region_11.12 | reduce | flops 3670016 | bytes 9437186 | tf_op jit(solution)/shard_map/reduce_sum | solution.py:12
  292.0 4.5 %fusion.22 = f32[64,16,512]{2,1,0:T(8,128)} fusion(bf16[64,16,512]{2,1,0:T(8,128)(2,1)S(1)} %bitcast.85, bf16[512,1024]{1,0:T(8,128)(2,1)S(1)} %reduce_sum.129, bf16[512,1024]{1,0:T(8,128)(2,1)S(1)} %copy-done, f32[512,512]{1,0:T(8,128)} %get-tuple-element.13), kind=kOutput, calls=%fused_computation.40 | convolution fusion | flops 1076363264 | bytes 6291456 | tf_op jit(solution)/shard_map/rd,rh->dh/dot_general | solution.py:185
  296.5 10.9 %all-to-all-start.3 = ((f32[64,16,512]{2,1,0:T(8,128)}), f32[64,16,512]{2,1,0:T(8,128)S(1)}, u32[]{:S(2)}, u32[]{:S(2)}) async-start(f32[64,16,512]{2,1,0:T(8,128)} %fusion.22), calls=%async_computation.3 | async-start | bytes 4194304 | tf_op jit(solution)/shard_map/all_to_all | solution.py:67
  307.4 2.3 copy.42
  309.7 3.4 fusion.29
  313.1 45.6 %all-to-all-done.3 = f32[64,16,512]{2,1,0:T(8,128)S(1)} async-done(((f32[64,16,512]{2,1,0:T(8,128)}), f32[64,16,512]{2,1,0:T(8,128)S(1)}, u32[]{:S(2)}, u32[]{:S(2)}) %all-to-all-start.3) | async-done | bytes 2097184 | tf_op jit(solution)/shard_map/all_to_all | solution.py:67
  358.7 5.6 %all-to-all-start.4 = ((f32[64,16,512]{2,1,0:T(8,128)}), f32[64,16,512]{2,1,0:T(8,128)}, u32[]{:S(2)}, u32[]{:S(2)}) async-start(f32[64,16,512]{2,1,0:T(8,128)} %fusion.29), calls=%async_computation.4 | async-start | bytes 4194304 | tf_op jit(solution)/shard_map/all_to_all | solution.py:67
  364.3 0.8 reduce_sum.130
  365.1 50.4 %all-to-all-done.4 = f32[64,16,512]{2,1,0:T(8,128)} async-done(((f32[64,16,512]{2,1,0:T(8,128)}), f32[64,16,512]{2,1,0:T(8,128)}, u32[]{:S(2)}, u32[]{:S(2)}) %all-to-all-start.4) | async-done | bytes 2097184 | tf_op jit(solution)/shard_map/all_to_all | solution.py:67
  415.5 2.3 reduce_sum.131
  (48 shorter events, 1.2 us)
Async XLA Ops:
  7.2 50.1 %copy-start = (bf16[512,1024]{1,0:T(8,128)(2,1)S(1)}, bf16[512,1024]{1,0:T(8,128)(2,1)}, u32[]{:S(2)}) copy-start(bf16[512,1024]{1,0:T(8,128)(2,1)} %param.18) | copy-start | bytes 3145732
  7.2 65.0 %all-gather.9.cloned.1.call-start = ((), (), s32[]{:S(2)}) async-start(), calls=%async_computation.7 | async-start | bytes 3244032 | tf_op jit(solution)/shard_map/all_gather | solution.py:109
  7.9 116.9 %reduce-scatter.4.cloned.1.call-start = ((), (), s32[]{:S(2)}) async-start(), calls=%async_computation.9 | async-start | bytes 1179648 | tf_op jit(solution)/shard_map/reduce_scatter | solution.py:39
  10.9 43.1 %copy-start.12 = (f32[1024]{0:T(1024)S(1)}, f32[1024]{0:T(1024)}, u32[]{:S(2)}) copy-start(f32[1024]{0:T(1024)} %param.16) | copy-start | bytes 12292
  53.4 1.2 copy-start.14
  54.6 1.8 copy-start.8
  56.5 0.8 copy-start.10
  72.1 2.7 copy-start.1
  74.5 1.2 copy-start.11
  83.8 2.5 copy-start.13
  86.2 3.1 copy-start.2
  89.3 1.1 copy-start.15
  98.1 76.4 %all-to-all-start.1 = ((bf16[8,512,176]{1,2,0:T(8,128)(2,1)}), bf16[8,512,176]{1,2,0:T(8,128)(2,1)S(1)}, u32[]{:S(2)}, u32[]{:S(2)}) async-start(bf16[8,512,176]{1,2,0:T(8,128)(2,1)} %broadcast_in_dim.17), calls=%async_computation.1 | async-start | bytes 2883584 | tf_op jit(solution)/shard_map/all_to_all | solution.py:23
  102.3 67.4 %all-gather.7.cloned.1.call-start = ((), (), s32[]{:S(2)}) async-start(), calls=%async_computation.6 | async-start | bytes 1179648 | tf_op jit(solution)/shard_map/all_gather | solution.py:42
  174.5 1.6 copy-start.3
  174.5 1.6 copy-start.6
  176.2 0.7 copy-start.5
  176.2 14.6 %copy-start.7 = (bf16[176,1024]{1,0:T(8,128)(2,1)S(1)}, bf16[176,1024]{1,0:T(8,128)(2,1)}, u32[]{:S(2)}) copy-start(bf16[176,1024]{1,0:T(8,128)(2,1)} %param.19) | copy-start | bytes 1081348
  177.5 12.5 %all-to-all-start.2 = ((f32[8,1,1536]{2,1,0:T(1,128)}), f32[8,1,1536]{2,1,0:T(1,128)S(1)}, u32[]{:S(2)}, u32[]{:S(2)}) async-start(f32[8,1,1536]{2,1,0:T(1,128)} %broadcast_in_dim.18), calls=%async_computation.2 | async-start | bytes 98304 | tf_op jit(solution)/shard_map/all_to_all | solution.py:23
  181.9 104.4 %all-gather.11.cloned.1.call-start = ((), (), s32[]{:S(2)}) async-start(), calls=%async_computation.8 | async-start | bytes 9437184 | tf_op jit(solution)/shard_map/all_gather | solution.py:12
  286.2 5.8 %copy-start.9 = (bf16[512,1024]{0,1:T(8,128)(2,1)S(1)}, bf16[512,1024]{0,1:T(8,128)(2,1)}, u32[]{:S(2)}) copy-start(bf16[512,1024]{0,1:T(8,128)(2,1)} %copy-done.8) | copy-start | bytes 3145732
  292.0 4.5 %copy-start.4 = (bf16[512,1024]{1,0:T(8,128)(2,1)}, bf16[512,1024]{1,0:T(8,128)(2,1)S(1)}, u32[]{:S(2)}) copy-start(bf16[512,1024]{1,0:T(8,128)(2,1)S(1)} %reduce_sum.129) | copy-start | bytes 3145732
  296.5 62.2 %all-to-all-start.3 = ((f32[64,16,512]{2,1,0:T(8,128)}), f32[64,16,512]{2,1,0:T(8,128)S(1)}, u32[]{:S(2)}, u32[]{:S(2)}) async-start(f32[64,16,512]{2,1,0:T(8,128)} %fusion.22), calls=%async_computation.3 | async-start | bytes 4194304 | tf_op jit(solution)/shard_map/all_to_all | solution.py:67
  358.7 56.8 %all-to-all-start.4 = ((f32[64,16,512]{2,1,0:T(8,128)}), f32[64,16,512]{2,1,0:T(8,128)}, u32[]{:S(2)}, u32[]{:S(2)}) async-start(f32[64,16,512]{2,1,0:T(8,128)} %fusion.29), calls=%async_computation.4 | async-start | bytes 4194304 | tf_op jit(solution)/shard_map/all_to_all | solution.py:67
Sparse Core Ops, SparseCore 0:
  10.1 61.9 all-gather.8
  75.0 49.8 reduce-scatter.3
  126.9 42.7 all-gather.6
  193.3 92.8 all-gather.10
